TPU v7x, 32 devices: a whole 2x2x4 slice. The times are simulated.
32 devices in a mesh: people: 2 (over x), tm: 8 (over z, y), type: 2 (over core).
Axes of the slice: x: 2, y: 2, z: 4, core: 2. Of those that a mesh axis runs over, the one named last changes fastest.
Arguments:
- features: bfloat16 [3, 2, 2048], P(None, 'people', 'tm'), may hold values from -6 to 6
- wear: int32 [2, 2048], P('people', 'tm'), may hold values 0 or 1
- rec_start: int32 [2], P('people'), may hold values from 0 to 255
- rec_end: int32 [2], P('people'), may hold values from 1793 to 2048
- conv_first: bfloat16 [3, 3, 128], replicated, may hold values from -2 to 2
- conv_second: bfloat16 [3, 128, 128], replicated, may hold values from -0.3125 to 0.3125
- emit_weight: bfloat16 [128, 512], P(None, 'type'), may hold values from -0.5 to 0.5
- leave: float32 [8, 64], P('type'), may hold values from 0.002 to 0.5
- jump: float32 [8, 64, 64], P('type'), may hold values from -6 to 6
- init_logits: float32 [8, 64], P('type'), may hold values from -6 to 6
- type_prior: float32 [8], replicated, may hold values from -4 to 4
Outputs:
- loglik_rate: float32 [2, 8], P('people', 'type')
- type_post: float32 [2, 8], P('people', 'type')
- occupancy: float32 [8, 64], P('type')
- filtered: float32 [2, 2048, 8, 64], P('people', 'tm', 'type')
All inputs are finite; a program needn't handle non-finite values. No bound on the sum of `wear` on one device may be relied on, other than what follows from the above.
Results may differ from a plain program's by a relative error of at most 0.0085.
Values may be sent and summed in bfloat16 or wider, within the bound.
A program may use at most 64 MiB of HBM per device.

v0:
```python
import jax
import jax.numpy as jnp
from jax import lax
from jax.sharding import PartitionSpec as P

HIGH = lax.Precision.HIGHEST


def padded(block, sides, width):
    for axis, dim in sides:
        count = lax.axis_size(axis)
        forward = [(i, i + 1) for i in range(count - 1)]
        backward = [(target, source) for source, target in forward]
        low = lax.ppermute(
            lax.slice_in_dim(block, block.shape[dim] - width, None, axis=dim), axis, forward
        )
        high = lax.ppermute(lax.slice_in_dim(block, 0, width, axis=dim), axis, backward)
        block = jnp.concatenate([low, block, high], axis=dim)
    return block


def prefix(shard, axis, combine, identity):
    size, mine = (lax.axis_size(axis), lax.axis_index(axis))
    everything = jax.tree.map(
        lambda part, kind: lax.all_gather(part.astype(kind), axis),
        shard,
        (jnp.bfloat16, jnp.bfloat16),
    )
    start = jax.tree.map(
        lambda part, zero: jnp.broadcast_to(jnp.asarray(zero, part.dtype), part.shape),
        shard,
        identity,
    )

    def turn(k, before):
        reached = k < mine
        new = combine(
            before, jax.tree.map(lambda part, own: part[k].astype(own.dtype), everything, shard)
        )
        return jax.tree.map(lambda a, b: jnp.where(reached, a, b), new, before)

    return lax.fori_loop(0, size, turn, start)


def chain_join(earlier, later):
    left, left_log = earlier
    right, right_log = later
    joined = jnp.einsum("...ij,...jk->...ik", left, right, precision=HIGH)
    scale = jnp.sum(joined, axis=(-2, -1)) / joined.shape[-1]
    return (joined / scale[..., None, None], left_log + right_log + jnp.log(scale))


def chain_product(mats, logs):
    while mats.shape[0] > 1:
        half = mats.shape[0] // 2
        joined, joined_log = chain_join(
            (mats[0 : 2 * half : 2], logs[0 : 2 * half : 2]),
            (mats[1 : 2 * half : 2], logs[1 : 2 * half : 2]),
        )
        mats, logs = (joined, joined_log)
    return (mats[0], logs[0])


def on_device(
    features,
    wear,
    rec_start,
    rec_end,
    conv_first,
    conv_second,
    emit_weight,
    leave,
    jump,
    init_logits,
    type_prior,
):
    persons = features.shape[1]
    span = features.shape[2]
    kinds = jump.shape[0]
    states = jump.shape[-1]
    tm_index = lax.axis_index("tm")
    type_index = lax.axis_index("type")
    total_epochs = span * lax.axis_size("tm")
    extended = padded(features, (("tm", 2),), 5)
    first = jnp.zeros((persons, span + 8, conv_first.shape[2]), jnp.float32)
    for tap in range(3):
        first = first + jnp.einsum(
            "ipt,ic->ptc",
            extended[:, :, tap : tap + span + 8],
            conv_first[tap],
            preferred_element_type=jnp.float32,
        )
    wide_pos = tm_index * span - 4 + jnp.arange(span + 8, dtype=jnp.int32)
    inside = (wide_pos >= 0) & (wide_pos < total_epochs)
    first = jnp.where(inside[None, :, None], jax.nn.silu(first), 0.0).astype(jnp.bfloat16)
    second = jnp.zeros((persons, span, conv_second.shape[2]), jnp.float32)
    for tap in range(3):
        second = second + jnp.einsum(
            "ptc,cd->ptd",
            first[:, 4 * tap : 4 * tap + span],
            conv_second[tap],
            preferred_element_type=jnp.float32,
        )
    second = jax.nn.silu(second).astype(jnp.bfloat16)
    logits = jnp.einsum("ptc,cm->ptm", second, emit_weight, preferred_element_type=jnp.float32)
    probs = jnp.exp(jax.nn.log_softmax(logits.reshape(persons, span, kinds, states), axis=-1))
    positions = tm_index * span + jnp.arange(span, dtype=jnp.int32)
    observed = (
        (wear > 0)
        & (positions[None, :] >= rec_start[:, None])
        & (positions[None, :] < rec_end[:, None])
    )
    emis = jnp.where(observed[:, :, None, None], probs, jnp.float32(1.0))
    observed_f = observed.astype(jnp.float32)
    eye_small = jnp.eye(states, dtype=jnp.float32)
    trans = (1.0 - leave)[..., None] * eye_small + leave[..., None] * jax.nn.softmax(jump, axis=-1)
    start = jax.nn.softmax(init_logits, axis=-1)
    start_all = jnp.broadcast_to(start, (persons, kinds, states))
    group = span // 16
    emis_blocks = jnp.transpose(emis.reshape(persons, 16, group, kinds, states), (1, 2, 0, 3, 4))
    eye_all = jnp.broadcast_to(eye_small, (persons, kinds, states, states))
    zero_logs = jnp.zeros((persons, kinds), jnp.float32)

    def block_leaves(block):
        return trans[None, None] * block[..., None, :]

    def pass_one(carry, block):
        leaves = block_leaves(block)
        product = chain_product(leaves, jnp.zeros(leaves.shape[:3], jnp.float32))
        return (chain_join(carry, product), None)

    (stretch, stretch_log), _ = lax.scan(pass_one, (eye_all, zero_logs), emis_blocks)
    before, before_log = prefix((stretch, stretch_log), "tm", chain_join, (eye_all, zero_logs))
    vec = jnp.einsum("pki,pkij->pkj", start_all, before, precision=HIGH)
    vec_total = jnp.sum(vec, axis=-1)
    alpha_in = vec / vec_total[..., None]
    log_in = before_log + jnp.log(vec_total)

    def advance(carry, inputs):
        alpha_now, log_now, occupied = carry
        emis_now, mask_now = inputs
        pred = jnp.einsum("pki,kij->pkj", alpha_now, trans, precision=HIGH)
        unnorm = pred * emis_now
        step_total = jnp.sum(unnorm, axis=-1)
        alpha_next = unnorm / step_total[..., None]
        occupied = occupied + mask_now[:, None, None] * alpha_next
        return ((alpha_next, log_now + jnp.log(step_total), occupied), alpha_next)

    zero_occupied = jnp.zeros((persons, kinds, states), jnp.float32)
    (alpha_end, own_log, occupied), history = lax.scan(
        advance,
        (alpha_in, zero_logs, zero_occupied),
        (jnp.transpose(emis, (1, 0, 2, 3)), observed_f.T),
    )
    filtered = jnp.transpose(history, (1, 0, 2, 3))
    contribution = log_in + own_log - log_in
    summed = lax.psum(contribution, "tm")
    full = lax.all_gather(summed, "type", axis=1, tiled=True)
    rate_full = full / total_epochs
    post_full = jax.nn.softmax(type_prior[None, :] + 8.0 * rate_full, axis=-1)
    offset = type_index * kinds
    rate_own = lax.dynamic_slice(rate_full, (jnp.int32(0), offset), (persons, kinds))
    post_own = lax.dynamic_slice(post_full, (jnp.int32(0), offset), (persons, kinds))
    numer = jnp.einsum("pk,pks->ks", post_own, occupied, precision=HIGH)
    denom = jnp.einsum("pk,p->k", post_own, jnp.sum(observed_f, axis=1), precision=HIGH)
    numer, denom = lax.psum((numer, denom), ("people", "tm"))
    occupancy = numer / denom[:, None]
    return (rate_own, post_own, occupancy, filtered)


def solution(mesh):
    return jax.shard_map(
        on_device,
        mesh=mesh,
        in_specs=(
            P(None, "people", "tm"),
            P("people", "tm"),
            P("people"),
            P("people"),
            P(),
            P(),
            P(None, "type"),
            P("type", None),
            P("type", None, None),
            P("type", None),
            P(),
        ),
        out_specs=(
            P("people", "type"),
            P("people", "type"),
            P("type", None),
            P("people", "tm", "type", None),
        ),
        check_vma=False,
    )
```

profile of v0, /device:TPU:0, one launch (start us, length us, event | category | flops | bytes accessed | tf_op | source)
XLA Modules:
  0.0 671.9 jit_solution(15239699927580164286)
XLA Ops:
  1.5 4.9 collective-permute-start
  9.0 1.4 convert_reduce_fusion
  13.7 1.5 fusion.37
  23.3 1.7 exponential_select_fusion
  26.0 85.4 %while.46 = (s32[]{:T(128)}, f32[1,4,64,64]{2,3,1,0:T(8,128)S(1)}, f32[1,4]{1,0:T(1,128)S(1)}, f32[4,64,64]{2,1,0:T(8,128)S(1)}, f32[16,16,1,4,64]{4,3,1,2,0:T(4,128)S(1)}, /*index=5*/s32[]{:T(128)}, s32[]{:T(128)}) while((s32[]{:T(128)}, f32[1,4,64,64]{2,3,1,0:T(8,128)S(1)}, f32[1,4]{1,0:T(1,128)S(1)}, ...), condition=%wide.region_10.11_spmd.clone, body=%wide.region_4.0_spmd.clone.sunk | while | flops 202113104 | bytes 6277803 | solution.py:132
  26.3 1.4 fusion.97
  31.6 1.4 fusion.97
  36.9 1.4 fusion.97
  42.3 1.4 fusion.97
  47.6 1.4 fusion.97
  53.0 1.4 fusion.97
  58.3 1.4 fusion.97
  63.6 1.4 fusion.97
  69.0 1.4 fusion.97
  95.7 1.4 fusion.97
  101.0 1.4 fusion.97
  106.4 1.4 fusion.97
  111.5 33.8 %all-gather = bf16[8,4,64,64]{3,2,1,0:T(8,128)(2,1)S(1)} all-gather(bf16[1,4,64,64]{3,2,1,0:T(8,128)(2,1)S(1)} %copy.52), channel_id=2, replica_groups=mesh['people'=2,'tm'=8,'type'=2] {'tm'}, dimensions={0}, use_global_device_ids=true | all-gather | bytes 294912 | tf_op jit(solution)/shard_map/all_gather | solution.py:25
  145.4 19.3 %all-gather.2 = bf16[8,1,4]{2,1,0:T(2,128)(2,1)S(1)} all-gather(bf16[1,1,4]{2,1,0:T(2,128)(2,1)S(1)} %convert_bitcast_fusion.1), channel_id=3, replica_groups=mesh['people'=2,'tm'=8,'type'=2] {'tm'}, dimensions={0}, use_global_device_ids=true | all-gather | bytes 72 | tf_op jit(solution)/shard_map/all_gather | solution.py:25
  164.7 4.1 while.47
  169.3 438.0 %while.48 = (s32[]{:T(128)}, f32[1,4,64]{2,1,0:T(4,128)S(1)}, f32[1,4]{1,0:T(1,128)S(1)}, f32[1,4,64]{2,1,0:T(4,128)S(1)}, f32[256,1,4,64]{3,2,1,0:T(4,128)S(1)}...) while((s32[]{:T(128)}, f32[1,4,64]{2,1,0:T(4,128)S(1)}, ...), condition=%wide.region_19.20_spmd.clone, body=%wide.region_17.19_spmd.clone.sunk | while | flops 198407 | bytes 81608 | solution.py:150
  607.3 17.1 %psum.21 = f32[1,4]{1,0:T(1,128)S(1)} all-reduce(f32[1,4]{1,0:T(1,128)S(1)} %add_subtract_fusion), channel_id=1, replica_groups=mesh['people'=2,'tm'=8,'type'=2] {'tm'}, use_global_device_ids=true, to_apply=%region_20.21 | all-reduce | flops 4 | bytes 32 | tf_op jit(solution)/shard_map/psum | solution.py:157
  625.5 2.4 all-reduce
  631.9 39.4 %all-reduce.1 = (f32[4,64]{1,0:T(4,128)S(1)}, f32[4]{0:T(128)S(1)}) all-reduce(f32[4,64]{1,0:T(4,128)S(1)} %bitcast_multiply_fusion.1, f32[4]{0:T(128)S(1)} %get-tuple-element.317), channel_id=1, replica_groups=mesh['people'=2,'tm'=8,'type'=2] {'people','tm'}, use_global_device_ids=true, to_apply=%region_23.24 | all-reduce | flops 260 | bytes 2080 | tf_op jit(solution)/shard_map/psum | solution.py:166
  (2064 shorter events, 523.4 us)
Async XLA Ops:
  0.6 21.3 %copy-start = (bf16[128,256]{1,0:T(8,128)(2,1)S(1)}, bf16[128,256]{1,0:T(8,128)(2,1)}, u32[]{:S(2)}) copy-start(bf16[128,256]{1,0:T(8,128)(2,1)} %param.23) | copy-start | bytes 196612
  0.6 21.1 %copy-start.1 = (bf16[3,128,128]{2,1,0:T(8,128)(2,1)S(1)}, bf16[3,128,128]{2,1,0:T(8,128)(2,1)}, u32[]{:S(2)}) copy-start(bf16[3,128,128]{2,1,0:T(8,128)(2,1)} %param.22) | copy-start | bytes 294916
  1.5 15.7 %collective-permute-start = (bf16[3,1,5]{2,0,1:T(4,128)(2,1)S(1)}, bf16[3,1,5]{2,0,1:T(4,128)(2,1)S(1)}, u32[]{:S(2)}, u32[]{:S(2)}) collective-permute-start(bf16[3,1,5]{2,0,1:T(4,128)(2,1)S(1)} %get-tuple-element.343), channel_id=1, source_target_pairs={{0,2},{2,4},{4,6},{6,8},{8,10},{10,12},{12,14},{1,3},{3,5},{5,7},{... | collective-permute-start | bytes 98 | tf_op jit(solution)/shard_map/ppermute | solution.py:14
  6.4 10.8 %collective-permute-start.1 = (bf16[3,1,5]{2,0,1:T(4,128)(2,1)S(1)}, bf16[3,1,5]{2,0,1:T(4,128)(2,1)S(1)}, u32[]{:S(2)}, u32[]{:S(2)}) collective-permute-start(bf16[3,1,5]{2,0,1:T(4,128)(2,1)S(1)} %get-tuple-element.344), channel_id=1, source_target_pairs={{2,0},{4,2},{6,4},{8,6},{10,8},{12,10},{14,12},{3,1},{5,3},{7,5},{... | collective-permute-start | bytes 98 | tf_op jit(solution)/shard_map/ppermute | solution.py:17
  164.7 463.2 %copy-start.3 = (f32[8]{0:T(128)S(1)}, f32[8]{0:T(128)}, u32[]{:S(2)}) copy-start(f32[8]{0:T(128)} %param.27) | copy-start | bytes 100
  631.8 40.1 %copy-start.2 = (f32[1,4]{1,0:T(1,128)}, f32[1,4]{1,0:T(1,128)S(1)}, u32[]{:S(2)}) copy-start(f32[1,4]{1,0:T(1,128)S(1)} %get-tuple-element.318) | copy-start | bytes 52
where the time goes:
time: 678 us; the launch traced here: 672 us
  other arithmetic  254 us (37%)
  local copies, waits for them, and re-layouts  168 us (25%)
  matrix products  121 us (18%)
  blocking collectives  112 us (17%)
  loops' own time  7.58 us (1%)
    add x256, other arithmetic, advance(): occupied = occupied + mask_now[:, None, None] * alpha_next  168 us
    dynamic_slice x256, local copies, waits for them, and re-layouts, on_device(): lax.scan(advance, (alpha_in, zero_logs, zero_occupied), (jnp.transpose(em...  151 us
    dot_general x88, matrix products, chain_join(): joined = jnp.einsum('...ij,...jk->...ik', left, right, precision=HIGH)  59.5 us
    dot_general x256, matrix products, advance(): pred = jnp.einsum('pki,kij->pkj', alpha_now, trans, precision=HIGH)  57.3 us
    all_gather x2, blocking collectives, prefix(): lax.all_gather(part.astype(kind), axis)  53.1 us
    psum x1, blocking collectives, on_device(): numer, denom = lax.psum((numer, denom), ('people', 'tm'))  39.4 us
    reduce_sum x256, other arithmetic, advance(): step_total = jnp.sum(unnorm, axis=-1)  30.6 us
    dynamic_update_slice x256, other arithmetic, on_device(): lax.scan(advance, (alpha_in, zero_logs, zero_occupied), (jnp.transpose(em...  21.8 us
  transfers between devices with their start and end apart: 2, of which 0 were waited for; matrix products, arithmetic and copies ran while one was open for 1% of the time, Pallas kernels for 0%

commit v1 on v0

v1 whole, which is shorter than its diff:
```python
import functools

import jax
import jax.numpy as jnp
from jax import lax
from jax.experimental import pallas as pl
from jax.experimental.pallas import tpu as pltpu
from jax.sharding import PartitionSpec as P

MESH = pl.DeviceIdType.MESH
F32 = jnp.float32
BF16 = jnp.bfloat16
CHUNKS = 16


def split2(x):
    hi = x.astype(BF16)
    return hi, (x - hi.astype(F32)).astype(BF16)


def dot(a, b):
    return jnp.dot(a, b, preferred_element_type=F32)


def silu(x):
    return x / (1.0 + jnp.exp(-x))


def kernel(
    sizes,
    feat_ref,
    wear_ref,
    rs_ref,
    re_ref,
    cf_ref,
    cs_ref,
    ew_ref,
    leave_ref,
    jump_ref,
    init_ref,
    prior_ref,
    rate_ref,
    post_ref,
    occ_ref,
    filt_ref,
    fbuf,
    halo_l,
    halo_r,
    w9,
    lj,
    tcat,
    rows,
    emis,
    seen,
    x_scr,
    q_scr,
    d_own,
    d_all,
    msg,
    stats,
    halo_send,
    halo_recv,
    d_send,
    d_recv,
    s_send,
    s_recv,
):
    n_p, n_t, n_k = sizes
    span = feat_ref.shape[2]
    kinds, states = leave_ref.shape
    width = kinds * states
    halves = width // 128
    group = CHUNKS
    steps = span // group
    me_p = lax.axis_index("people")
    me_t = lax.axis_index("tm")
    me_k = lax.axis_index("type")
    others = [
        (a, b, c)
        for b in range(n_t)
        for a in range(n_p)
        for c in range(n_k)
        if (a, b, c) != (0, 0, 0)
    ]

    barrier = pltpu.get_barrier_semaphore()
    for a, b, c in others:
        pl.semaphore_signal(
            barrier,
            inc=1,
            device_id=(
                lax.rem(me_p + a, n_p),
                lax.rem(me_t + b, n_t),
                lax.rem(me_k + c, n_k),
            ),
            device_id_type=MESH,
        )

    fbuf[...] = jnp.zeros_like(fbuf)
    for i in range(feat_ref.shape[0]):
        fbuf[i : i + 1, :] = feat_ref[i].astype(F32)

    pl.semaphore_wait(barrier, len(others))
    right = lax.rem(me_t + 1, n_t)
    left = lax.rem(me_t + n_t - 1, n_t)
    to_right = pltpu.make_async_remote_copy(
        src_ref=fbuf.at[:, span - 128 : span],
        dst_ref=halo_l,
        send_sem=halo_send.at[0],
        recv_sem=halo_recv.at[0],
        device_id=(me_p, right, me_k),
        device_id_type=MESH,
    )
    to_left = pltpu.make_async_remote_copy(
        src_ref=fbuf.at[:, 0:128],
        dst_ref=halo_r,
        send_sem=halo_send.at[1],
        recv_sem=halo_recv.at[1],
        device_id=(me_p, left, me_k),
        device_id_type=MESH,
    )
    to_right.start()
    to_left.start()

    r64 = lax.broadcasted_iota(jnp.int32, (states, states), 0)
    c64 = lax.broadcasted_iota(jnp.int32, (states, states), 1)
    eye64 = r64 == c64
    rw = lax.broadcasted_iota(jnp.int32, (width, width), 0)
    cw = lax.broadcasted_iota(jnp.int32, (width, width), 1)
    ones_blk = jnp.where(rw // states == cw // states, 1.0, 0.0).astype(BF16)
    eye_cat = (
        lax.broadcasted_iota(jnp.int32, (states, width), 1) % states
        == lax.broadcasted_iota(jnp.int32, (states, width), 0)
    )

    lj[...] = jnp.zeros_like(lj)
    rows[...] = jnp.zeros_like(rows)
    for k in range(kinds):
        lanes = slice(k * states, (k + 1) * states)
        logit = jump_ref[k]
        e = jnp.exp(logit - jnp.max(logit, axis=1, keepdims=True))
        soft = e / jnp.sum(e, axis=1, keepdims=True)
        away = leave_ref[k : k + 1, :]
        away_col = jnp.sum(jnp.where(eye64, away, 0.0), axis=1, keepdims=True)
        jumped = away_col * soft
        lj[lanes, lanes] = jumped
        tcat[:, lanes] = jumped + jnp.where(eye64, 1.0 - away, 0.0)
        rows[0:1, lanes] = 1.0 - away
        first_logit = init_ref[k : k + 1, :]
        e0 = jnp.exp(first_logit - jnp.max(first_logit, axis=1, keepdims=True))
        rows[1:2, lanes] = e0 / jnp.sum(e0, axis=1, keepdims=True)
    lj_b = lj[...].astype(BF16)
    both = jnp.concatenate([lj_b, ones_blk], axis=1)
    stay = rows[0:1, :]

    def blocksum(x):
        hi, lo = split2(x)
        return dot(hi, ones_blk) + dot(lo, ones_blk)

    place = me_t * span + lax.broadcasted_iota(jnp.int32, (1, span), 1)
    seen_row = (wear_ref[...] > 0) & (place >= rs_ref[0]) & (place < re_ref[0])
    seen_row = jnp.where(seen_row, 1.0, 0.0)
    re_ = lax.broadcasted_iota(jnp.int32, (span, span), 0)
    ce_ = lax.broadcasted_iota(jnp.int32, (span, span), 1)
    seen_diag = jnp.where(re_ == ce_, seen_row, 0.0).astype(BF16)
    seen[...] = dot(seen_diag, jnp.ones((span, 128), BF16))

    w9[...] = jnp.zeros_like(w9)
    for j in range(3):
        w9[8 * j : 8 * j + cf_ref.shape[1], :] = cf_ref[j].astype(F32)

    to_right.wait()
    to_left.wait()
    before = jnp.where(me_t > 0, halo_l[...], 0.0)
    after = jnp.where(me_t < n_t - 1, halo_r[...], 0.0)
    ext = jnp.concatenate([before, fbuf[...], after], axis=1)
    wide = span + 128
    taps = jnp.concatenate([ext[:, 123 + j : 123 + j + wide] for j in range(3)], axis=0)
    first = lax.dot_general(
        taps.T.astype(BF16), w9[...].astype(BF16), (((1,), (0,)), ((), ())),
        preferred_element_type=F32,
    )
    first = silu(first[0 : span + 8])
    wpos = me_t * span - 4 + lax.broadcasted_iota(jnp.int32, first.shape, 0)
    first = jnp.where((wpos >= 0) & (wpos < span * n_t), first, 0.0)
    second = (
        dot(first[0:span].astype(BF16), cs_ref[0])
        + dot(first[4 : span + 4].astype(BF16), cs_ref[1])
        + dot(first[8 : span + 8].astype(BF16), cs_ref[2])
    )
    second = silu(second).astype(BF16)
    logits = dot(second, ew_ref[...])
    tops = [
        jnp.broadcast_to(
            jnp.max(logits[:, k * states : (k + 1) * states], axis=1, keepdims=True),
            (span, states),
        )
        for k in range(kinds)
    ]
    raw = jnp.exp(logits - jnp.concatenate(tops, axis=1))
    obs = jnp.concatenate([seen[...]] * halves, axis=1)
    log_part = -jnp.sum(obs * jnp.log(blocksum(raw)), axis=0, keepdims=True)
    raw = jnp.where(obs > 0.0, raw, 1.0)
    for h in range(halves):
        emis[h] = raw[:, h * 128 : (h + 1) * 128]

    def emission(step):
        at = pl.ds(step, group, stride=steps)
        return jnp.concatenate([emis[h, at, :] for h in range(halves)], axis=1)


    tc = tcat[...]

    def col(x):
        return jnp.sum(x.reshape(group, states, width), axis=1)

    e_first = emission(0)
    x0 = (tc[None] * e_first[:, None, :]).reshape(group * states, width)
    x_scr[...] = x0

    def grow(step, total):
        scale = 1.0 / dot(total.astype(BF16), ones_blk)
        e_now = emission(step) * scale
        x = x_scr[...]
        moved = dot(x.astype(BF16), lj_b) + x * stay
        x = (moved.reshape(group, states, width) * e_now[:, None, :]).reshape(
            group * states, width
        )
        x_scr[...] = x
        return col(x)

    total = lax.fori_loop(1, steps, grow, col(x0))

    q_scr[0] = jnp.where(eye_cat, 1.0, 0.0)
    q = x_scr[0:states, :]
    block_mask = rw // states == cw // states

    def as_block(x):
        return jnp.where(block_mask, jnp.concatenate([x] * kinds, axis=0), 0.0)

    for g in range(1, group):
        scale = 1.0 / dot(
            jnp.broadcast_to(jnp.sum(q, axis=0, keepdims=True), (8, width)).astype(BF16), ones_blk
        )
        q_scr[g] = q
        p_hi, p_lo = split2(as_block(x_scr[g * states : (g + 1) * states, :]))
        q_hi, q_lo = split2(q)
        moved = dot(jnp.concatenate([q_hi, q_lo], axis=0), p_hi)
        q = (moved[0:states] + moved[states:] + dot(q_hi, p_lo)) * scale[0:1]
    scale = 1.0 / dot(
            jnp.broadcast_to(jnp.sum(q, axis=0, keepdims=True), (8, width)).astype(BF16), ones_blk
        )
    d_own[...] = (q * scale[0:1]).astype(BF16)

    def send_operator(b):
        return pltpu.make_async_remote_copy(
            src_ref=d_own,
            dst_ref=d_all.at[me_t],
            send_sem=d_send.at[b],
            recv_sem=d_recv.at[me_t],
            device_id=(me_p, lax.rem(me_t + b, n_t), me_k),
            device_id_type=MESH,
        )

    for b in range(1, n_t):
        @pl.when(me_t + b < n_t)
        def _():
            send_operator(b).start()

    def expand(v):
        hi, lo = split2(jnp.where(eye_cat, v, 0.0))
        return dot(hi, ones_blk) + dot(lo, ones_blk)

    def apply(d, v):
        pltpu.make_async_remote_copy(
            src_ref=d_own,
            dst_ref=d_all.at[d],
            send_sem=d_send.at[0],
            recv_sem=d_recv.at[d],
            device_id=(me_p, left, me_k),
            device_id_type=MESH,
        ).wait_recv()
        spread = expand(v)
        new = jnp.sum(spread * d_all[d].astype(F32), axis=0, keepdims=True)
        return new / jnp.sum(spread, axis=0, keepdims=True)

    alpha_in = lax.fori_loop(0, me_t, apply, rows[1:2, :])

    spread = expand(alpha_in)
    alpha0 = jnp.concatenate(
        [jnp.sum(spread * q_scr[g], axis=0, keepdims=True) for g in range(group)], axis=0
    )

    def forward(u):
        hi, lo = split2(u)
        got = dot(jnp.concatenate([hi, lo], axis=0), both)
        got = got[0:group] + got[group:]
        return u * stay + got[:, :width], 1.0 / got[:, width:]

    logs = jnp.zeros((group, width), F32)
    occupied = jnp.zeros((group, width), F32)
    ahead, inv = forward(alpha0)
    for step in range(steps):
        u = ahead * inv * emission(step)
        ahead, inv = forward(u)
        alpha = u * inv
        for k in range(kinds):
            half = alpha[:, k // 2 * 128 : k // 2 * 128 + 128]
            filt_ref[pl.ds(step * kinds + k, group, stride=steps * kinds), :] = (
                half if k % 2 == 0 else pltpu.roll(half, 64, 1)
            )
        mask = seen[pl.ds(step, group, stride=steps), :]
        mask = jnp.concatenate([mask] * halves, axis=1)
        logs = logs - jnp.log(inv)
        occupied = occupied + mask * alpha

    loglik = jnp.sum(logs, axis=0, keepdims=True) + log_part
    occupied = jnp.sum(occupied, axis=0, keepdims=True)

    msg[...] = jnp.zeros_like(msg)
    for h in range(halves):
        lanes = slice(h * 128, (h + 1) * 128)
        msg[h : h + 1, :] = occupied[:, lanes]
        msg[2 + h : 3 + h, :] = loglik[:, lanes]
    count = jnp.sum(seen_row, axis=1, keepdims=True)
    msg[4:5, :] = jnp.broadcast_to(count, (1, 128))
    own = (me_p * n_k + me_k) * n_t + me_t

    def send_sums(a, b, c):
        return pltpu.make_async_remote_copy(
            src_ref=msg,
            dst_ref=stats.at[own],
            send_sem=s_send,
            recv_sem=s_recv,
            device_id=(
                lax.rem(me_p + a, n_p),
                lax.rem(me_t + b, n_t),
                lax.rem(me_k + c, n_k),
            ),
            device_id_type=MESH,
        )

    sends = [send_sums(*o) for o in others]
    for s in sends:
        s.start()
    stats[own] = msg[...]
    for b in range(1, n_t):
        @pl.when(me_t + b < n_t)
        def _():
            send_operator(b).wait_send()
    most = pl.ds(0, len(others))
    pltpu.make_async_copy(stats.at[most], stats.at[most], s_send).wait()
    pltpu.make_async_copy(stats.at[most], stats.at[most], s_recv).wait()

    sums = [
        [
            jnp.sum(stats[(p * n_k + c) * n_t : (p * n_k + c + 1) * n_t], axis=0)
            for c in range(n_k)
        ]
        for p in range(n_p)
    ]
    lane = lax.broadcasted_iota(jnp.int32, (1, 128), 1)
    epochs = float(span * n_t)

    def over_types(op, parts):
        m = functools.reduce(op, parts)
        return op(m, pltpu.roll(m, 64, 1))

    numer = [jnp.zeros((1, 128), F32) for _ in range(halves)]
    denom = [jnp.zeros((1, 128), F32) for _ in range(halves)]
    for p in range(n_p):
        rates, tempered = [], []
        for c in range(n_k):
            for h in range(halves):
                base = c * kinds + 2 * h
                rate = sums[p][c][2 + h : 3 + h, :] / epochs
                rates.append(rate)
                prior = jnp.where(lane < states, prior_ref[base], prior_ref[base + 1])
                tempered.append(prior + 8.0 * rate)
        top = over_types(jnp.maximum, tempered)
        weights = [jnp.exp(x - top) for x in tempered]
        whole = over_types(jnp.add, weights)
        for h in range(halves):
            post = functools.reduce(
                jnp.add,
                [
                    jnp.where(me_k == c, weights[c * halves + h] / whole, 0.0)
                    for c in range(n_k)
                ],
            )
            rate = functools.reduce(
                jnp.add,
                [jnp.where(me_k == c, rates[c * halves + h], 0.0) for c in range(n_k)],
            )
            occ = functools.reduce(
                jnp.add,
                [jnp.where(me_k == c, sums[p][c][h : h + 1, :], 0.0) for c in range(n_k)],
            )
            numer[h] = numer[h] + post * occ
            denom[h] = denom[h] + post * sums[p][0][4:5, :]
            rows[2 + h : 3 + h, 0:128] = jnp.where(me_p == p, rate, rows[2 + h : 3 + h, 0:128])
            rows[4 + h : 5 + h, 0:128] = jnp.where(me_p == p, post, rows[4 + h : 5 + h, 0:128])
    for k in range(kinds):
        h, at = k // 2, (k % 2) * states
        rate_ref[0:1, k : k + 1] = rows[2 + h : 3 + h, at : at + 1]
        post_ref[0:1, k : k + 1] = rows[4 + h : 5 + h, at : at + 1]
        occ_ref[k : k + 1, :] = (numer[h] / denom[h])[:, at : at + states]


def on_device(sizes, features, *rest):
    jump = rest[7]
    kinds, states = jump.shape[0], jump.shape[2]
    span = features.shape[2]
    width = kinds * states
    n_p, n_t, n_k = sizes
    vmem = pl.BlockSpec(memory_space=pltpu.VMEM)
    smem = pl.BlockSpec(memory_space=pltpu.SMEM)
    rate, post, occ, filt = pl.pallas_call(
        functools.partial(kernel, sizes),
        out_shape=(
            jax.ShapeDtypeStruct((1, kinds), F32),
            jax.ShapeDtypeStruct((1, kinds), F32),
            jax.ShapeDtypeStruct((kinds, states), F32),
            jax.ShapeDtypeStruct((span * kinds, 128), F32),
        ),
        in_specs=[vmem, vmem, smem, smem, vmem, vmem, vmem, vmem, vmem, vmem, smem],
        out_specs=(vmem, vmem, vmem, vmem),
        scratch_shapes=[
            pltpu.VMEM((8, span), F32),
            pltpu.VMEM((8, 128), F32),
            pltpu.VMEM((8, 128), F32),
            pltpu.VMEM((24, 128), F32),
            pltpu.VMEM((width, width), F32),
            pltpu.VMEM((states, width), F32),
            pltpu.VMEM((8, width), F32),
            pltpu.VMEM((width // 128, span, 128), F32),
            pltpu.VMEM((span, 128), F32),
            pltpu.VMEM((CHUNKS * states, width), F32),
            pltpu.VMEM((CHUNKS, states, width), F32),
            pltpu.VMEM((states, width), BF16),
            pltpu.VMEM((n_t, states, width), BF16),
            pltpu.VMEM((8, 128), F32),
            pltpu.VMEM((n_p * n_t * n_k, 8, 128), F32),
            pltpu.SemaphoreType.DMA((2,)),
            pltpu.SemaphoreType.DMA((2,)),
            pltpu.SemaphoreType.DMA((n_t,)),
            pltpu.SemaphoreType.DMA((n_t,)),
            pltpu.SemaphoreType.DMA,
            pltpu.SemaphoreType.DMA,
        ],
        compiler_params=pltpu.CompilerParams(
            collective_id=0, has_side_effects=True, vmem_limit_bytes=40 * 1024 * 1024
        ),
    )(features, *rest)
    return rate, post, occ, filt[:, :states].reshape(1, span, kinds, states)


def solution(mesh):
    sizes = (mesh.shape["people"], mesh.shape["tm"], mesh.shape["type"])
    return jax.shard_map(
        functools.partial(on_device, sizes),
        mesh=mesh,
        in_specs=(
            P(None, "people", "tm"),
            P("people", "tm"),
            P("people"),
            P("people"),
            P(),
            P(),
            P(None, "type"),
            P("type", None),
            P("type", None, None),
            P("type", None),
            P(),
        ),
        out_specs=(
            P("people", "type"),
            P("people", "type"),
            P("type", None),
            P("people", "tm", "type", None),
        ),
        check_vma=False,
    )
```

time: 678 us -> 45.9 us (0.07)
  other arithmetic: 254 us -> 0 us
  local copies, waits for them, and re-layouts: 168 us -> 5.86 us
  matrix products: 121 us -> 0 us
  blocking collectives: 112 us -> 0 us
  Pallas kernels: 0 us -> 37.7 us
  loops' own time: 7.58 us -> 0 us
    add x576 -> x0, other arithmetic: 175 us -> none  [the longest x256 168 us: advance(): occupied = occupied + mask_now[:, None, None] * alpha_next]
    dynamic_slice x257 -> x0, local copies, waits for them, and re-layouts: 152 us -> none  [the longest x256 151 us: on_device(): lax.scan(advance, (alpha_in, zero_logs, zero_occupied), (jnp.transpose(em...]
    dot_general x351 -> x0, matrix products: 121 us -> none  [the longest x88 59.5 us: chain_join(): joined = jnp.einsum('...ij,...jk->...ik', left, right, precision=HIGH)]
    psum x2 -> x0, blocking collectives: 56.5 us -> none  [the longest x1 39.4 us: on_device(): numer, denom = lax.psum((numer, denom), ('people', 'tm'))]
    all_gather x2 -> x0, blocking collectives: 53.1 us -> none  [prefix(): lax.all_gather(part.astype(kind), axis)]
    pallas_call x0 -> x1, Pallas kernels: none -> 37.7 us  [on_device(): pl.pallas_call(functools.partial(kernel, sizes), out_shape=(jax.ShapeDtyp...]
    reduce_sum x261 -> x0, other arithmetic: 34.3 us -> none  [the longest x256 30.6 us: advance(): step_total = jnp.sum(unnorm, axis=-1)]
    dynamic_update_slice x256 -> x0, other arithmetic: 21.8 us -> none  [on_device(): lax.scan(advance, (alpha_in, zero_logs, zero_occupied), (jnp.transpose(em...]
  transfers between devices with their start and end apart: 2 -> 0, of which waited for: 0 -> 0; matrix products, arithmetic and copies ran while one was open for 1% -> 0% of each run, Pallas kernels for 0% -> 0%
where the time goes in v1:
time: 45.9 us; the launch traced here: 45.6 us
  Pallas kernels  37.7 us (82%)
  local copies, waits for them, and re-layouts  5.86 us (13%)
  between operations  2.04 us (4%)
    pallas_call x1, Pallas kernels, on_device(): pl.pallas_call(functools.partial(kernel, sizes), out_shape=(jax.ShapeDtyp...  37.7 us
    unnamed x21, local copies, waits for them, and re-layouts  5.86 us

profile of v1, /device:TPU:0, one launch (start us, length us, event | category | flops | bytes accessed | tf_op | source)
XLA Modules:
  0.0 45.6 jit_solution(16653627677604914735)
XLA Ops:
  0.6 0.0 copy-start.5
  1.3 0.0 copy-start.3
  2.0 0.0 copy-start.4
  2.0 0.0 copy-start.6
  2.0 0.0 copy-start.7
  2.0 0.7 %copy.15.feat_ref = bf16[3,1,256]{2,1,0:T(2,128)(2,1)S(1)} copy(bf16[3,1,256]{2,0,1:T(4,128)(2,1)} %param.11) | data formatting | bytes 3072 | tf_op args[0]
  2.7 0.0 copy-done.5
  2.7 0.0 copy-done.3
  2.7 0.0 copy-done.4
  2.7 0.0 copy-done.6
  2.7 0.0 copy-done.7
  2.7 0.0 copy-start
  2.8 0.9 %copy-done = f32[4,64,64]{2,1,0:T(8,128)S(1)} copy-done((f32[4,64,64]{2,1,0:T(8,128)S(1)}, f32[4,64,64]{2,1,0:T(8,128)}, u32[]{:S(2)}) %copy-start) | copy-done | bytes 65560
  3.7 0.0 copy-start.1
  3.7 0.9 %copy-done.1 = bf16[3,128,128]{2,1,0:T(8,128)(2,1)S(1)} copy-done((bf16[3,128,128]{2,1,0:T(8,128)(2,1)S(1)}, bf16[3,128,128]{2,1,0:T(8,128)(2,1)}, u32[]{:S(2)}) %copy-start.1) | copy-done | bytes 98328
  4.5 0.0 copy-start.2
  4.5 0.8 %copy-done.2 = bf16[128,256]{1,0:T(8,128)(2,1)S(1)} copy-done((bf16[128,256]{1,0:T(8,128)(2,1)S(1)}, bf16[128,256]{1,0:T(8,128)(2,1)}, u32[]{:S(2)}) %copy-start.2) | copy-done | bytes 65560
  5.4 37.7 %shard_map.138 = (f32[1,4]{1,0:T(1,128)S(1)}, f32[1,4]{1,0:T(1,128)S(1)}, f32[4,64]{1,0:T(4,128)S(1)}, f32[1024,128]{1,0:T(8,128)S(1)}) custom-call(bf16[3,1,256]{2,1,0:T(2,128)(2,1)S(1)} %copy.15.feat_ref, s32[1,256]{1,0:T(1,128)S(1)} %copy-done.6, s32[1]{0:T(128)S(6)} %copy.20.rs_ref, s32[1]{0:T(128)S(6)} %copy.21.re_ref, ...), custom_call_target="tpu_custom_call" | custom-call | tf_op jit(solution)/shard_map/pallas_call | solution.py:418
  43.1 0.9 %copy.16 = f32[1,256,4,64]{1,3,2,0:T(8,128)} copy(f32[1,256,4,64]{3,2,1,0:T(4,128)S(1)} %bitcast.2) | data formatting | bytes 524288
  44.0 0.5 %copy.22 = f32[1,4]{1,0:T(1,128)} copy(f32[1,4]{1,0:T(1,128)S(1)} %get-tuple-element.20) | data formatting | bytes 32
  44.5 0.5 %copy.23 = f32[1,4]{1,0:T(1,128)} copy(f32[1,4]{1,0:T(1,128)S(1)} %get-tuple-element.21) | data formatting | bytes 32
  45.1 0.6 %copy.24 = f32[4,64]{1,0:T(4,128)} copy(f32[4,64]{1,0:T(4,128)S(1)} %get-tuple-element.22) | data formatting | bytes 2048
Async XLA Ops:
  0.6 2.1 %copy-start.5 = (f32[4,64]{1,0:T(4,128)S(1)}, f32[4,64]{1,0:T(4,128)}, u32[]{:S(2)}) copy-start(f32[4,64]{1,0:T(4,128)} %init_ref.1) | copy-start | bytes 3076
  1.3 1.4 %copy-start.3 = (bf16[3,3,128]{2,1,0:T(4,128)(2,1)S(1)}, bf16[3,3,128]{2,1,0:T(4,128)(2,1)}, u32[]{:S(2)}) copy-start(bf16[3,3,128]{2,1,0:T(4,128)(2,1)} %cf_ref.1) | copy-start | bytes 6916
  2.0 0.7 %copy-start.4 = (f32[4,64]{1,0:T(4,128)S(1)}, f32[4,64]{1,0:T(4,128)}, u32[]{:S(2)}) copy-start(f32[4,64]{1,0:T(4,128)} %leave_ref.1) | copy-start | bytes 3076
  2.0 0.7 %copy-start.6 = (s32[1,256]{1,0:T(1,128)S(1)}, s32[1,256]{1,0:T(1,128)}, u32[]{:S(2)}) copy-start(s32[1,256]{1,0:T(1,128)} %wear_ref.1) | copy-start | bytes 3076
  2.0 0.7 %copy-start.7 = (f32[8]{0:T(128)S(1)}, f32[8]{0:T(128)}, u32[]{:S(2)}) copy-start(f32[8]{0:T(128)} %prior_ref.1) | copy-start | bytes 100
  2.7 0.9 %copy-start = (f32[4,64,64]{2,1,0:T(8,128)S(1)}, f32[4,64,64]{2,1,0:T(8,128)}, u32[]{:S(2)}) copy-start(f32[4,64,64]{2,1,0:T(8,128)} %jump_ref.1) | copy-start | bytes 196612
  3.7 0.9 %copy-start.1 = (bf16[3,128,128]{2,1,0:T(8,128)(2,1)S(1)}, bf16[3,128,128]{2,1,0:T(8,128)(2,1)}, u32[]{:S(2)}) copy-start(bf16[3,128,128]{2,1,0:T(8,128)(2,1)} %cs_ref.1) | copy-start | bytes 294916
  4.5 0.8 %copy-start.2 = (bf16[128,256]{1,0:T(8,128)(2,1)S(1)}, bf16[128,256]{1,0:T(8,128)(2,1)}, u32[]{:S(2)}) copy-start(bf16[128,256]{1,0:T(8,128)(2,1)} %ew_ref.1) | copy-start | bytes 196612

commit v2 on v1

--- a/solution.py
+++ b/solution.py
@@ -33,10 +33,10 @@
     rs_ref,
     re_ref,
     cf_ref,
-    cs_ref,
-    ew_ref,
+    cs_any,
+    ew_any,
     leave_ref,
-    jump_ref,
+    jump_any,
     init_ref,
     prior_ref,
     rate_ref,
@@ -64,6 +64,10 @@
     d_recv,
     s_send,
     s_recv,
+    cs_ref,
+    ew_ref,
+    jump_ref,
+    loads,
 ):
     n_p, n_t, n_k = sizes
     span = feat_ref.shape[2]
@@ -83,6 +87,13 @@
         if (a, b, c) != (0, 0, 0)
     ]
 
+    fetch_jump = pltpu.make_async_copy(jump_any, jump_ref, loads.at[0])
+    fetch_cs = pltpu.make_async_copy(cs_any, cs_ref, loads.at[1])
+    fetch_ew = pltpu.make_async_copy(ew_any, ew_ref, loads.at[2])
+    fetch_jump.start()
+    fetch_cs.start()
+    fetch_ew.start()
+
     barrier = pltpu.get_barrier_semaphore()
     for a, b, c in others:
         pl.semaphore_signal(
@@ -135,6 +146,7 @@
 
     lj[...] = jnp.zeros_like(lj)
     rows[...] = jnp.zeros_like(rows)
+    fetch_jump.wait()
     for k in range(kinds):
         lanes = slice(k * states, (k + 1) * states)
         logit = jump_ref[k]
@@ -169,6 +181,8 @@
     for j in range(3):
         w9[8 * j : 8 * j + cf_ref.shape[1], :] = cf_ref[j].astype(F32)
 
+    fetch_cs.wait()
+    fetch_ew.wait()
     to_right.wait()
     to_left.wait()
     before = jnp.where(me_t > 0, halo_l[...], 0.0)
@@ -414,6 +428,7 @@
     width = kinds * states
     n_p, n_t, n_k = sizes
     vmem = pl.BlockSpec(memory_space=pltpu.VMEM)
+    hbm = pl.BlockSpec(memory_space=pl.ANY)
     smem = pl.BlockSpec(memory_space=pltpu.SMEM)
     rate, post, occ, filt = pl.pallas_call(
         functools.partial(kernel, sizes),
@@ -423,7 +438,7 @@
             jax.ShapeDtypeStruct((kinds, states), F32),
             jax.ShapeDtypeStruct((span * kinds, 128), F32),
         ),
-        in_specs=[vmem, vmem, smem, smem, vmem, vmem, vmem, vmem, vmem, vmem, smem],
+        in_specs=[vmem, vmem, smem, smem, vmem, hbm, hbm, vmem, hbm, vmem, smem],
         out_specs=(vmem, vmem, vmem, vmem),
         scratch_shapes=[
             pltpu.VMEM((8, span), F32),
@@ -447,6 +462,10 @@
             pltpu.SemaphoreType.DMA((n_t,)),
             pltpu.SemaphoreType.DMA,
             pltpu.SemaphoreType.DMA,
+            pltpu.VMEM(rest[4].shape, BF16),
+            pltpu.VMEM(rest[5].shape, BF16),
+            pltpu.VMEM(jump.shape, F32),
+            pltpu.SemaphoreType.DMA((3,)),
         ],
         compiler_params=pltpu.CompilerParams(
             collective_id=0, has_side_effects=True, vmem_limit_bytes=40 * 1024 * 1024

time: 45.9 us -> 46.4 us (1.011)
  Pallas kernels: 37.7 us -> 38.2 us
where the time goes in v2:
time: 46.4 us; the launch traced here: 46.1 us
  Pallas kernels  38.2 us (82%)
  local copies, waits for them, and re-layouts  5.86 us (13%)
  between operations  2.04 us (4%)
    pallas_call x1, Pallas kernels, on_device(): pl.pallas_call(functools.partial(kernel, sizes), out_shape=(jax.ShapeDtyp...  38.2 us
    unnamed x21, local copies, waits for them, and re-layouts  5.86 us

profile of v2, /device:TPU:0, one launch (start us, length us, event | category | flops | bytes accessed | tf_op | source)
XLA Modules:
  0.0 46.1 jit_solution(12659775834853088467)
XLA Ops:
  0.6 0.0 copy-start.5
  1.3 0.0 copy-start.3
  2.0 0.0 copy-start.4
  2.0 0.0 copy-start.6
  2.0 0.0 copy-start.7
  2.0 0.7 %copy.15.feat_ref = bf16[3,1,256]{2,1,0:T(2,128)(2,1)S(1)} copy(bf16[3,1,256]{2,0,1:T(4,128)(2,1)} %param.11) | data formatting | bytes 3072 | tf_op args[0]
  2.7 0.0 copy-done.5
  2.7 0.0 copy-done.3
  2.7 0.0 copy-done.4
  2.7 0.0 copy-done.6
  2.7 0.0 copy-done.7
  2.7 0.0 copy-start
  2.8 0.9 %copy-done = f32[4,64,64]{2,1,0:T(8,128)S(1)} copy-done((f32[4,64,64]{2,1,0:T(8,128)S(1)}, f32[4,64,64]{2,1,0:T(8,128)}, u32[]{:S(2)}) %copy-start) | copy-done | bytes 65560
  3.7 0.0 copy-start.1
  3.7 0.9 %copy-done.1 = bf16[3,128,128]{2,1,0:T(8,128)(2,1)S(1)} copy-done((bf16[3,128,128]{2,1,0:T(8,128)(2,1)S(1)}, bf16[3,128,128]{2,1,0:T(8,128)(2,1)}, u32[]{:S(2)}) %copy-start.1) | copy-done | bytes 98328
  4.5 0.0 copy-start.2
  4.5 0.8 %copy-done.2 = bf16[128,256]{1,0:T(8,128)(2,1)S(1)} copy-done((bf16[128,256]{1,0:T(8,128)(2,1)S(1)}, bf16[128,256]{1,0:T(8,128)(2,1)}, u32[]{:S(2)}) %copy-start.2) | copy-done | bytes 65560
  5.4 38.2 %shard_map.138 = (f32[1,4]{1,0:T(1,128)S(1)}, f32[1,4]{1,0:T(1,128)S(1)}, f32[4,64]{1,0:T(4,128)S(1)}, f32[1024,128]{1,0:T(8,128)S(1)}) custom-call(bf16[3,1,256]{2,1,0:T(2,128)(2,1)S(1)} %copy.15.feat_ref, s32[1,256]{1,0:T(1,128)S(1)} %copy-done.6, s32[1]{0:T(128)S(6)} %copy.20.rs_ref, s32[1]{0:T(128)S(6)} %copy.21.re_ref, ...), custom_call_target="tpu_custom_call" | custom-call | tf_op jit(solution)/shard_map/pallas_call | solution.py:433
  43.6 0.9 %copy.16 = f32[1,256,4,64]{1,3,2,0:T(8,128)} copy(f32[1,256,4,64]{3,2,1,0:T(4,128)S(1)} %bitcast.2) | data formatting | bytes 524288
  44.5 0.5 %copy.22 = f32[1,4]{1,0:T(1,128)} copy(f32[1,4]{1,0:T(1,128)S(1)} %get-tuple-element.20) | data formatting | bytes 32
  45.0 0.5 %copy.23 = f32[1,4]{1,0:T(1,128)} copy(f32[1,4]{1,0:T(1,128)S(1)} %get-tuple-element.21) | data formatting | bytes 32
  45.5 0.6 %copy.24 = f32[4,64]{1,0:T(4,128)} copy(f32[4,64]{1,0:T(4,128)S(1)} %get-tuple-element.22) | data formatting | bytes 2048
Async XLA Ops:
  0.6 2.1 %copy-start.5 = (f32[4,64]{1,0:T(4,128)S(1)}, f32[4,64]{1,0:T(4,128)}, u32[]{:S(2)}) copy-start(f32[4,64]{1,0:T(4,128)} %init_ref.1) | copy-start | bytes 3076
  1.3 1.4 %copy-start.3 = (bf16[3,3,128]{2,1,0:T(4,128)(2,1)S(1)}, bf16[3,3,128]{2,1,0:T(4,128)(2,1)}, u32[]{:S(2)}) copy-start(bf16[3,3,128]{2,1,0:T(4,128)(2,1)} %cf_ref.1) | copy-start | bytes 6916
  2.0 0.7 %copy-start.4 = (f32[4,64]{1,0:T(4,128)S(1)}, f32[4,64]{1,0:T(4,128)}, u32[]{:S(2)}) copy-start(f32[4,64]{1,0:T(4,128)} %leave_ref.1) | copy-start | bytes 3076
  2.0 0.7 %copy-start.6 = (s32[1,256]{1,0:T(1,128)S(1)}, s32[1,256]{1,0:T(1,128)}, u32[]{:S(2)}) copy-start(s32[1,256]{1,0:T(1,128)} %wear_ref.1) | copy-start | bytes 3076
  2.0 0.7 %copy-start.7 = (f32[8]{0:T(128)S(1)}, f32[8]{0:T(128)}, u32[]{:S(2)}) copy-start(f32[8]{0:T(128)} %prior_ref.1) | copy-start | bytes 100
  2.7 0.9 %copy-start = (f32[4,64,64]{2,1,0:T(8,128)S(1)}, f32[4,64,64]{2,1,0:T(8,128)}, u32[]{:S(2)}) copy-start(f32[4,64,64]{2,1,0:T(8,128)} %jump_any.1) | copy-start | bytes 196612
  3.7 0.9 %copy-start.1 = (bf16[3,128,128]{2,1,0:T(8,128)(2,1)S(1)}, bf16[3,128,128]{2,1,0:T(8,128)(2,1)}, u32[]{:S(2)}) copy-start(bf16[3,128,128]{2,1,0:T(8,128)(2,1)} %cs_any.1) | copy-start | bytes 294916
  4.5 0.8 %copy-start.2 = (bf16[128,256]{1,0:T(8,128)(2,1)S(1)}, bf16[128,256]{1,0:T(8,128)(2,1)}, u32[]{:S(2)}) copy-start(bf16[128,256]{1,0:T(8,128)(2,1)} %ew_any.1) | copy-start | bytes 196612
